TPU v7x, 32 devices: a whole 2x2x4 slice. The times are simulated.
32 devices in a mesh: groups: 2 (over y), row: 8 (over z, x), col: 2 (over core).
Axes of the slice: x: 2, y: 2, z: 4, core: 2. Of those that a mesh axis runs over, the one named last changes fastest.
Arguments:
- src_emb: bfloat16 [8192, 128], P(('groups', 'row', 'col')), parts along dimension 0, may hold values from -6 to 6
- tgt_emb: bfloat16 [65536, 128], P(('groups', 'col', 'row')), parts along dimension 0, may hold values from -6 to 6
- src_scale: float32 [8192], P(('groups', 'row', 'col')), parts along dimension 0, may hold values from 0.5 to 1.5
- tgt_scale: float32 [65536], P(('groups', 'col', 'row')), parts along dimension 0, may hold values from 0.5 to 1.5
- src_mass: float32 [8192], P(('groups', 'row')), parts along dimension 0, may hold values from 0.05 to 20
- tgt_mass: float32 [65536], P(('groups', 'col')), parts along dimension 0, may hold values from 0.05 to 20
Outputs:
- src_potential: float32 [8192], P(('groups', 'row')), parts along dimension 0
- tgt_potential: float32 [65536], P(('groups', 'col')), parts along dimension 0
There are 2 independent parts, one for each index of `groups`. A program takes and returns all parts, laid end to end along the dimension named above; each array names one. Nothing has to cross between parts.
All inputs are finite; a program needn't handle non-finite values.
Results may differ from a plain program's by a relative error of at most 0.00056.
Values may be sent and summed in bfloat16 or wider, within the bound.
A program may use at most 64 MiB of HBM per device.

v0:
```python
import jax
import jax.numpy as jnp
from jax import lax
from jax.sharding import PartitionSpec as P

ITERS = 3


EPSILON = 0.05


def unit_rows(emb, scale):
    values = emb.astype(jnp.float32)
    length = jnp.sqrt(jnp.sum(values * values, axis=1) + 1e-06)
    return (values * (scale / length)[:, None]).astype(jnp.bfloat16)


def make_tile(src_block, piece):
    scores = lax.dot_general(
        src_block, piece, (((1,), (1,)), ((), ())), preferred_element_type=jnp.float32
    )
    return jnp.exp(scores / EPSILON).astype(jnp.bfloat16)


def sum_rows(partial_rows):
    return lax.psum(partial_rows, "col")


def sum_cols(partial_cols):
    return lax.psum(partial_cols, "row")


def body(src_emb, tgt_emb, src_scale, tgt_scale, src_mass, tgt_mass):
    src_block = lax.all_gather(unit_rows(src_emb, src_scale), "col", axis=0, tiled=True)
    tgt_unit = unit_rows(tgt_emb, tgt_scale)
    left_scaling = jnp.ones((src_block.shape[0],), jnp.float32)
    kernel = make_tile(src_block, lax.all_gather(tgt_unit, "row", axis=0, tiled=True))
    right_scaling = jnp.ones((kernel.shape[1],), jnp.float32)
    for step in range(ITERS):
        partial_rows = jnp.dot(
            kernel, right_scaling.astype(jnp.bfloat16), preferred_element_type=jnp.float32
        )
        left_scaling = src_mass / sum_rows(partial_rows)
        partial_cols = jnp.dot(
            left_scaling.astype(jnp.bfloat16), kernel, preferred_element_type=jnp.float32
        )
        right_scaling = tgt_mass / sum_cols(partial_cols)
    return (EPSILON * jnp.log(left_scaling), EPSILON * jnp.log(right_scaling))


def solution(mesh):
    in_specs = (
        P(("groups", "row", "col"), None),
        P(("groups", "col", "row"), None),
        P(("groups", "row", "col")),
        P(("groups", "col", "row")),
        P(("groups", "row")),
        P(("groups", "col")),
    )
    out_specs = (P(("groups", "row")), P(("groups", "col")))
    return jax.shard_map(body, mesh=mesh, in_specs=in_specs, out_specs=out_specs, check_vma=False)
```

profile of v0, /device:TPU:0, one launch (start us, length us, event | category | flops | bytes accessed | tf_op | source)
XLA Modules:
  0.0 376.9 jit_solution(7758739568218210169)
XLA Ops:
  7.2 0.0 all-gather.2.cloned.1.call-start
  7.2 1.4 fusion
  8.6 0.7 rsqrt_multiply_fusion
  9.3 2.2 fusion.1
  11.5 0.0 all-gather.2.cloned.1.call-update
  11.5 0.0 all-reduce.4.cloned.1.call-start
  11.6 1.0 fusion.2
  12.5 0.7 rsqrt_multiply_fusion.1
  13.2 0.9 fusion.3
  14.1 2.0 all_gather.6
  16.1 0.0 copy-start.1
  16.1 71.6 %all-gather.2.cloned.1.call-done = bf16[16384,128]{1,0:T(8,128)(2,1)} async-done(((bf16[2048,128]{1,0:T(8,128)(2,1)}), bf16[16384,128]{1,0:T(8,128)(2,1)}) %all-gather.2.cloned.1.call-update) | async-done | bytes 4194320 | tf_op jit(solution)/shard_map/all_gather | solution.py:37
  87.8 10.2 %exponential_convert_fusion = bf16[512,16384]{1,0:T(8,128)(2,1)} fusion(bf16[512,128]{1,0:T(8,128)(2,1)S(1)} %all_gather.6, bf16[16384,128]{1,0:T(8,128)(2,1)} %all-gather.2.cloned.1.call-done), kind=kOutput, calls=%fused_computation | convolution fusion | flops 2164260864 | bytes 21102592 | tf_op jit(solution)/shard_map/dot_general | solution.py:19
  98.0 0.0 copy-start
  98.0 10.2 %fusion.4 = f32[1,512]{1,0:T(1,128)S(1)} fusion(bf16[512,16384]{1,0:T(8,128)(2,1)} %exponential_convert_fusion), kind=kOutput, calls=%fused_computation.12 | convolution fusion | flops 16777216 | bytes 16779264 | tf_op jit(solution)/shard_map/dot_general | solution.py:40
  108.2 2.5 psum.42
  110.7 0.0 copy-done.1
  110.7 8.7 %fusion.7 = f32[1,16384]{1,0:T(1,128)} fusion(bf16[512,1]{0,1:T(2,128)(2,1)S(1)} %reshape.8, bf16[512,16384]{1,0:T(8,128)(2,1)} %exponential_convert_fusion), kind=kOutput, calls=%fused_computation.21 | convolution fusion | flops 16777216 | bytes 16843776 | tf_op jit(solution)/shard_map/dot_general | solution.py:44
  119.4 0.0 all-reduce.4.cloned.1.call-update
  119.4 0.2 all-reduce.6.cloned.1.call-start
  119.6 66.7 %all-reduce.4.cloned.1.call-done = f32[16384]{0:T(1024)} async-done(((f32[16384]{0:T(1024)}), f32[16384]{0:T(1024)}) %all-reduce.4.cloned.1.call-update) | async-done | bytes 65552 | tf_op jit(solution)/shard_map/psum | solution.py:30
  186.3 0.0 copy-done
  186.3 0.9 divide_convert_fusion.1
  187.2 10.2 %fusion.8 = f32[1,512]{1,0:T(1,128)S(1)} fusion(bf16[512,16384]{1,0:T(8,128)(2,1)} %exponential_convert_fusion, bf16[16384,1]{0,1:T(2,128)(2,1)S(1)} %reshape.10), kind=kOutput, calls=%fused_computation.22 | convolution fusion | flops 16777216 | bytes 16812032 | tf_op jit(solution)/shard_map/dot_general | solution.py:40
  197.4 2.5 psum.44
  199.9 8.7 %fusion.9 = f32[1,16384]{1,0:T(1,128)} fusion(bf16[512,1]{0,1:T(2,128)(2,1)S(1)} %reshape.12, bf16[512,16384]{1,0:T(8,128)(2,1)} %exponential_convert_fusion), kind=kOutput, calls=%fused_computation.23 | convolution fusion | flops 16777216 | bytes 16843776 | tf_op jit(solution)/shard_map/dot_general | solution.py:44
  208.5 0.0 all-reduce.6.cloned.1.call-update
  208.6 0.0 all-reduce.8.cloned.1.call-start
  208.6 68.6 %all-reduce.6.cloned.1.call-done = f32[16384]{0:T(1024)} async-done(((f32[16384]{0:T(1024)}), f32[16384]{0:T(1024)}) %all-reduce.6.cloned.1.call-update) | async-done | bytes 65552 | tf_op jit(solution)/shard_map/psum | solution.py:30
  277.2 0.9 divide_convert_fusion
  278.1 10.2 %fusion.10 = f32[1,512]{1,0:T(1,128)S(1)} fusion(bf16[512,16384]{1,0:T(8,128)(2,1)} %exponential_convert_fusion, bf16[16384,1]{0,1:T(2,128)(2,1)S(1)} %reshape.14), kind=kOutput, calls=%fused_computation.24 | convolution fusion | flops 16777216 | bytes 16812032 | tf_op jit(solution)/shard_map/dot_general | solution.py:40
  288.3 2.7 psum.46
  290.9 0.6 divide_convert_fusion.4
  291.5 8.7 %fusion.11 = f32[1,16384]{1,0:T(1,128)} fusion(bf16[512,1]{0,1:T(2,128)(2,1)S(1)} %reshape.16, bf16[512,16384]{1,0:T(8,128)(2,1)} %exponential_convert_fusion), kind=kOutput, calls=%fused_computation.25 | convolution fusion | flops 16777216 | bytes 16843776 | tf_op jit(solution)/shard_map/dot_general | solution.py:44
  300.2 0.0 all-reduce.8.cloned.1.call-update
  300.2 68.6 %all-reduce.8.cloned.1.call-done = f32[16384]{0:T(1024)} async-done(((f32[16384]{0:T(1024)}), f32[16384]{0:T(1024)}) %all-reduce.8.cloned.1.call-update) | async-done | bytes 65552 | tf_op jit(solution)/shard_map/psum | solution.py:30
  368.9 1.5 log_multiply_fusion
  (7 shorter events, 0.1 us)
Async XLA Ops:
  7.2 80.6 %all-gather.2.cloned.1.call-start = ((), (), s32[]{:S(2)}) async-start(), calls=%async_computation | async-start | bytes 4718592 | tf_op jit(solution)/shard_map/all_gather | solution.py:37
  11.5 174.8 %all-reduce.4.cloned.1.call-start = ((), (), s32[]{:S(2)}) async-start(), calls=%async_computation.1 | async-start | bytes 131072 | tf_op jit(solution)/shard_map/psum | solution.py:30
  16.1 94.5 %copy-start.1 = (f32[512]{0:T(512)S(1)}, f32[512]{0:T(512)}, u32[]{:S(2)}) copy-start(f32[512]{0:T(512)} %param.10) | copy-start | bytes 6148
  98.0 88.3 %copy-start = (f32[16384]{0:T(1024)S(1)}, f32[16384]{0:T(1024)}, u32[]{:S(2)}) copy-start(f32[16384]{0:T(1024)} %param.11) | copy-start | bytes 196612
  119.4 157.8 %all-reduce.6.cloned.1.call-start = ((), (), s32[]{:S(2)}) async-start(), calls=%async_computation.2 | async-start | bytes 131072 | tf_op jit(solution)/shard_map/psum | solution.py:30
  208.6 160.3 %all-reduce.8.cloned.1.call-start = ((), (), s32[]{:S(2)}) async-start(), calls=%async_computation.3 | async-start | bytes 131072 | tf_op jit(solution)/shard_map/psum | solution.py:30
Sparse Core Ops, SparseCore 0:
  11.6 76.0 all-gather.1
  119.5 66.7 all-reduce.3
  208.7 68.4 all-reduce.5
  300.4 68.4 all-reduce.7
where the time goes:
time: 378 us; the launch traced here: 377 us
  waiting for transfers between devices  276 us (73%)
  matrix products  66.8 us (18%)
  between operations  13.8 us (4%)
  other arithmetic  10.7 us (3%)
  blocking collectives  9.6 us (3%)
    psum x3, waiting for transfers between devices, sum_cols(): return lax.psum(partial_cols, 'row')  204 us
    all_gather x1, waiting for transfers between devices, body(): lax.all_gather(tgt_unit, 'row', axis=0, tiled=True)  71.6 us
    dot_general x3, matrix products, body(): jnp.dot(kernel, right_scaling.astype(jnp.bfloat16), preferred_element_typ...  30.6 us
    dot_general x3, matrix products, body(): jnp.dot(left_scaling.astype(jnp.bfloat16), kernel, preferred_element_type...  26 us
    dot_general x1, matrix products, make_tile(): lax.dot_general(src_block, piece, (((1,), (1,)), ((), ())), preferred_ele...  10.2 us
    psum x3, blocking collectives, sum_rows(): return lax.psum(partial_rows, 'col')  7.6 us
  transfers between devices with their start and end apart: 4, of which 4 were waited for; matrix products, arithmetic and copies ran while one was open for 1% of the time, Pallas kernels for 0%

commit v1 on v0

v1 whole, which is shorter than its diff:
```python
import jax
import jax.numpy as jnp
from jax import lax
from jax.sharding import PartitionSpec as P

ITERS = 3


EPSILON = 0.05


def unit_rows(emb, scale):
    values = emb.astype(jnp.float32)
    length = jnp.sqrt(jnp.sum(values * values, axis=1) + 1e-06)
    return (values * (scale / length)[:, None]).astype(jnp.bfloat16)


def body(src_emb, tgt_emb, src_scale, tgt_scale, src_mass, tgt_mass):
    both = ("row", "col")
    src_all = lax.all_gather(unit_rows(src_emb, src_scale), both, axis=0, tiled=True)
    mass_all = lax.all_gather(src_mass, "row", axis=0, tiled=True)
    tgt_unit = unit_rows(tgt_emb, tgt_scale)
    own = tgt_unit.shape[0]
    row = lax.axis_index("row")
    mass_own = lax.dynamic_slice(tgt_mass, (row * own,), (own,))
    scores = lax.dot_general(
        src_all, tgt_unit, (((1,), (1,)), ((), ())), preferred_element_type=jnp.float32
    )
    kernel = jnp.exp(scores / EPSILON).astype(jnp.bfloat16)
    right_scaling = jnp.ones((own,), jnp.float32)
    for step in range(ITERS):
        partial_rows = jnp.dot(
            kernel, right_scaling.astype(jnp.bfloat16), preferred_element_type=jnp.float32
        )
        left_scaling = mass_all / lax.psum(partial_rows, both)
        cols = jnp.dot(
            left_scaling.astype(jnp.bfloat16), kernel, preferred_element_type=jnp.float32
        )
        right_scaling = mass_own / cols
    rows_own = src_mass.shape[0]
    left_own = lax.dynamic_slice(left_scaling, (row * rows_own,), (rows_own,))
    right_all = lax.all_gather(EPSILON * jnp.log(right_scaling), "row", axis=0, tiled=True)
    return (EPSILON * jnp.log(left_own), right_all)


def solution(mesh):
    in_specs = (
        P(("groups", "row", "col"), None),
        P(("groups", "col", "row"), None),
        P(("groups", "row", "col")),
        P(("groups", "col", "row")),
        P(("groups", "row")),
        P(("groups", "col")),
    )
    out_specs = (P(("groups", "row")), P(("groups", "col")))
    return jax.shard_map(body, mesh=mesh, in_specs=in_specs, out_specs=out_specs, check_vma=False)
```

time: 378 us -> 325 us (0.86)
  waiting for transfers between devices: 276 us -> 11 us
  blocking collectives: 9.6 us -> 234 us
  matrix products: 66.8 us -> 49.5 us
  local copies, waits for them, and re-layouts: 0.1 us -> 7.26 us
    psum x3 -> x0, waiting for transfers between devices: 204 us -> none  [sum_cols(): return lax.psum(partial_cols, 'row')]
    psum x3, blocking collectives: 7.6 us -> 175 us  [body(): left_scaling = mass_all / lax.psum(partial_rows, both)]
    all_gather x1, waiting for transfers between devices: 71.6 us -> 10.9 us  [body(): lax.all_gather(unit_rows(src_emb, src_scale), both, axis=0, tiled=True)]
    all_gather x1 -> x2, blocking collectives: 2 us -> 58.4 us  [the longest x1 30.5 us: body(): lax.all_gather(EPSILON * jnp.log(right_scaling), 'row', axis=0, tiled=True)]
    dot_general x3, matrix products: 30.6 us -> 19 us  [body(): jnp.dot(kernel, right_scaling.astype(jnp.bfloat16), preferred_element_typ...]
    unnamed x4 -> x5, local copies, waits for them, and re-layouts: 0.01 us -> 7.2 us
    dot_general x1, matrix products: 10.2 us -> 6.24 us  [body(): lax.dot_general(src_all, tgt_unit, (((1,), (1,)), ((), ())), preferred_el...]
  transfers between devices with their start and end apart: 4 -> 1, of which waited for: 4 -> 1; matrix products, arithmetic and copies ran while one was open for 1% -> 1% of each run, Pallas kernels for 0% -> 0%
where the time goes in v1:
time: 325 us; the launch traced here: 324 us
  blocking collectives  234 us (72%)
  matrix products  49.5 us (15%)
  between operations  14.1 us (4%)
  waiting for transfers between devices  11 us (3%)
  other arithmetic  8.87 us (3%)
  local copies, waits for them, and re-layouts  7.26 us (2%)
    psum x3, blocking collectives, body(): left_scaling = mass_all / lax.psum(partial_rows, both)  175 us
    all_gather x1, blocking collectives, body(): lax.all_gather(EPSILON * jnp.log(right_scaling), 'row', axis=0, tiled=True)  30.5 us
    all_gather x1, blocking collectives, body(): mass_all = lax.all_gather(src_mass, 'row', axis=0, tiled=True)  27.9 us
    dot_general x3, matrix products, body(): jnp.dot(left_scaling.astype(jnp.bfloat16), kernel, preferred_element_type...  24.3 us
    dot_general x3, matrix products, body(): jnp.dot(kernel, right_scaling.astype(jnp.bfloat16), preferred_element_typ...  19 us
    all_gather x1, waiting for transfers between devices, body(): lax.all_gather(unit_rows(src_emb, src_scale), both, axis=0, tiled=True)  10.9 us
    unnamed x5, local copies, waits for them, and re-layouts  7.2 us
  transfers between devices with their start and end apart: 1, of which 1 were waited for; matrix products, arithmetic and copies ran while one was open for 1% of the time, Pallas kernels for 0%

profile of v1, /device:TPU:0, one launch (start us, length us, event | category | flops | bytes accessed | tf_op | source)
XLA Modules:
  0.0 324.3 jit_solution(3006919935487138763)
XLA Ops:
  7.2 0.0 all-gather.3.cloned.1.call-start
  7.2 1.0 fusion.4
  8.2 0.7 rsqrt_multiply_fusion.1
  8.9 1.6 fusion.5
  10.4 0.0 all-gather.3.cloned.1.call-update
  10.5 27.9 %all-gather = f32[8,1,512]{2,1,0:T(1,128)S(1)} all-gather(f32[1,1,512]{2,1,0:T(1,128)} %bitcast.29), channel_id=1, replica_groups=mesh['groups'=2,'row'=8,'col'=2] {'row'}, dimensions={0}, use_global_device_ids=true | all-gather | bytes 18432 | tf_op jit(solution)/shard_map/all_gather | solution.py:21
  38.4 1.4 fusion
  39.8 0.7 rsqrt_multiply_fusion
  40.5 10.9 %all-gather.3.cloned.1.call-done = bf16[4096,128]{1,0:T(8,128)(2,1)} async-done(((bf16[256,128]{1,0:T(8,128)(2,1)}), bf16[4096,128]{1,0:T(8,128)(2,1)}) %all-gather.3.cloned.1.call-update) | async-done | bytes 1048592 | tf_op jit(solution)/shard_map/all_gather | solution.py:20
  51.4 6.2 %exponential_convert_fusion = bf16[4096,2048]{1,0:T(8,128)(2,1)S(1)} fusion(bf16[4096,128]{1,0:T(8,128)(2,1)} %all-gather.3.cloned.1.call-done, bf16[2048,128]{1,0:T(8,128)(2,1)} %param.7, f32[2048]{0:T(1024)S(1)} %rsqrt_multiply_fusion), kind=kOutput, calls=%fused_computation | convolution fusion | flops 2165047296 | bytes 18358272 | tf_op jit(solution)/shard_map/dot_general | solution.py:26
  57.7 0.0 copy-start
  57.7 5.7 %copy-done = bf16[4096,2048]{1,0:T(8,128)(2,1)} copy-done((bf16[4096,2048]{1,0:T(8,128)(2,1)}, bf16[4096,2048]{1,0:T(8,128)(2,1)S(1)}, u32[]{:S(2)}) %copy-start) | copy-done | bytes 16777240
  63.4 4.4 %fusion.6 = f32[1,4096]{1,0:T(1,128)S(1)} fusion(bf16[4096,2048]{1,0:T(8,128)(2,1)S(1)} %exponential_convert_fusion), kind=kOutput, calls=%fused_computation.16 | convolution fusion | flops 16777216 | bytes 16793600 | tf_op jit(solution)/shard_map/dot_general | solution.py:32
  67.8 59.6 %psum.21 = f32[4096]{0:T(1024)S(1)} all-reduce(f32[4096]{0:T(1024)S(1)} %bitcast.25), channel_id=1, replica_groups=mesh['groups'=2,'row'=8,'col'=2] {'row','col'}, use_global_device_ids=true, to_apply=%region_2.0 | all-reduce | flops 4096 | bytes 32768 | tf_op jit(solution)/shard_map/psum | solution.py:35
  127.4 0.0 copy-start.1
  127.5 8.2 %fusion.10 = f32[1,2048]{1,0:T(1,128)S(1)} fusion(bf16[4096,1]{0,1:T(2,128)(2,1)S(1)} %reshape.10, bf16[4096,2048]{1,0:T(8,128)(2,1)} %copy-done), kind=kOutput, calls=%fused_computation.22 | convolution fusion | flops 16777216 | bytes 16793600 | tf_op jit(solution)/shard_map/dot_general | solution.py:36
  135.7 1.5 divide_convert_fusion.3
  137.1 0.9 copy-done.1
  138.0 4.4 %fusion.11 = f32[1,4096]{1,0:T(1,128)S(1)} fusion(bf16[4096,2048]{1,0:T(8,128)(2,1)S(1)} %copy-done.1, bf16[2048,1]{0,1:T(2,128)(2,1)S(1)} %reshape.12), kind=kOutput, calls=%fused_computation.23 | convolution fusion | flops 16777216 | bytes 16797696 | tf_op jit(solution)/shard_map/dot_general | solution.py:32
  142.4 57.6 %psum.22 = f32[4096]{0:T(1024)S(1)} all-reduce(f32[4096]{0:T(1024)S(1)} %bitcast.23), channel_id=1, replica_groups=mesh['groups'=2,'row'=8,'col'=2] {'row','col'}, use_global_device_ids=true, to_apply=%region_3.0 | all-reduce | flops 4096 | bytes 32768 | tf_op jit(solution)/shard_map/psum | solution.py:35
  200.1 8.0 %fusion.12 = f32[1,2048]{1,0:T(1,128)S(1)} fusion(bf16[4096,1]{0,1:T(2,128)(2,1)S(1)} %reshape.14, bf16[4096,2048]{1,0:T(8,128)(2,1)} %copy-done), kind=kOutput, calls=%fused_computation.24 | convolution fusion | flops 16777216 | bytes 16793600 | tf_op jit(solution)/shard_map/dot_general | solution.py:36
  208.1 0.7 divide_convert_fusion.2
  208.8 10.2 %fusion.13 = f32[1,4096]{1,0:T(1,128)S(1)} fusion(bf16[4096,2048]{1,0:T(8,128)(2,1)} %copy-done, bf16[2048,1]{0,1:T(2,128)(2,1)S(1)} %reshape.16), kind=kOutput, calls=%fused_computation.25 | convolution fusion | flops 16777216 | bytes 16797696 | tf_op jit(solution)/shard_map/dot_general | solution.py:32
  219.0 57.8 %psum.23 = f32[4096]{0:T(1024)S(1)} all-reduce(f32[4096]{0:T(1024)S(1)} %bitcast.24), channel_id=1, replica_groups=mesh['groups'=2,'row'=8,'col'=2] {'row','col'}, use_global_device_ids=true, to_apply=%region_4.0 | all-reduce | flops 4096 | bytes 32768 | tf_op jit(solution)/shard_map/psum | solution.py:35
  276.9 8.0 %fusion.14 = f32[1,2048]{1,0:T(1,128)S(1)} fusion(bf16[4096,1]{0,1:T(2,128)(2,1)S(1)} %reshape.18, bf16[4096,2048]{1,0:T(8,128)(2,1)} %copy-done), kind=kOutput, calls=%fused_computation.26 | convolution fusion | flops 16777216 | bytes 16793600 | tf_op jit(solution)/shard_map/dot_general | solution.py:36
  284.9 0.7 log_multiply_fusion
  285.6 30.5 %all_gather.11 = f32[16384]{0:T(1024)S(1)} all-gather(f32[2048]{0:T(1024)S(1)} %log_multiply_fusion), channel_id=1, replica_groups=mesh['groups'=2,'row'=8,'col'=2] {'row'}, dimensions={0}, use_global_device_ids=true | all-gather | bytes 73728 | tf_op jit(solution)/shard_map/all_gather | solution.py:42
  316.1 0.7 log_multiply_fusion.1
  316.8 0.6 copy.9
  (8 shorter events, 0.1 us)
Async XLA Ops:
  7.2 44.3 %all-gather.3.cloned.1.call-start = ((), (), s32[]{:S(2)}) async-start(), calls=%async_computation | async-start | bytes 1114112 | tf_op jit(solution)/shard_map/all_gather | solution.py:20
  57.7 5.7 %copy-start = (bf16[4096,2048]{1,0:T(8,128)(2,1)}, bf16[4096,2048]{1,0:T(8,128)(2,1)S(1)}, u32[]{:S(2)}) copy-start(bf16[4096,2048]{1,0:T(8,128)(2,1)S(1)} %exponential_convert_fusion) | copy-start | bytes 50331652
  127.4 10.6 %copy-start.1 = (bf16[4096,2048]{1,0:T(8,128)(2,1)S(1)}, bf16[4096,2048]{1,0:T(8,128)(2,1)}, u32[]{:S(2)}) copy-start(bf16[4096,2048]{1,0:T(8,128)(2,1)} %copy-done) | copy-start | bytes 50331652
Sparse Core Ops, SparseCore 0:
  10.7 40.6 all-gather.2

commit v2 on v0

v2 whole, which is shorter than its diff:
```python
import functools
import jax
import jax.numpy as jnp
from jax import lax
from jax.experimental import pallas as pl
from jax.experimental.pallas import tpu as pltpu
from jax.sharding import PartitionSpec as P

ITERS = 3


EPSILON = 0.05
LOG2_E = 1.4426950408889634
MESH = pl.DeviceIdType.MESH
F32 = jnp.float32
BF16 = jnp.bfloat16


def unit_rows(emb, scale):
    values = emb.astype(F32)
    length = jnp.sqrt(jnp.sum(values * values, axis=1) + 1e-06)
    return (values * (scale / length)[:, None]).astype(BF16)


def lanes_to_row(acc):
    high = acc.astype(BF16)
    low = (acc - high.astype(F32)).astype(BF16)
    both = jnp.concatenate([high, low], axis=1)
    ones = jnp.ones((8, both.shape[1]), BF16)
    return lax.dot_general(
        ones, both, (((1,), (1,)), ((), ())), preferred_element_type=F32
    )


def sinkhorn(
    n_row, n_col,
    src_ref, tgt_ref, src_mass_ref, tgt_mass_ref,
    src_out, tgt_out,
    src_all, kernel, part, inbox, left, right,
    gather_send, gather_recv, sum_send, sum_recv, left_send, left_recv, out_send, out_recv,
):
    n_dev = n_row * n_col
    row, col = lax.axis_index("row"), lax.axis_index("col")
    me = row * n_col + col
    size = src_ref.shape[0]
    own = tgt_ref.shape[0]

    def rows_of(q):
        return pl.ds(pl.multiple_of(q * size, size), size)

    def after(k):
        return lax.rem(me + k, n_dev)

    def before(k):
        return lax.rem(me - k + n_dev, n_dev)

    def peer(q):
        return {"row": q // n_col, "col": lax.rem(q, n_col)}

    def copy(src, dst, send, recv, device):
        return pltpu.make_async_remote_copy(
            src_ref=src, dst_ref=dst, send_sem=send, recv_sem=recv,
            device_id=device, device_id_type=MESH,
        )

    def gather_copy(q, origin):
        return copy(src_ref, src_all.at[rows_of(origin), :],
                    gather_send.at[q], gather_recv.at[origin], peer(q))

    def sum_copy(q, origin):
        return copy(part.at[:, rows_of(q)], inbox.at[origin],
                    sum_send.at[q], sum_recv.at[origin], peer(q))

    def left_copy(q, origin):
        return copy(left.at[:, rows_of(origin)], left.at[:, rows_of(origin)],
                    left_send.at[q], left_recv.at[origin], peer(q))

    barrier = pltpu.get_barrier_semaphore()

    @pl.loop(1, n_dev)
    def _(k):
        pl.semaphore_signal(barrier, inc=1, device_id=peer(after(k)), device_id_type=MESH)

    pl.semaphore_wait(barrier, n_dev - 1)

    @pl.loop(1, n_dev)
    def _(k):
        q = after(k)
        gather_copy(q, me).start()

    def lane_sums(tile_of):
        acc = tile_of(0)
        for j in range(1, own // 128):
            acc = acc + tile_of(j)
        return acc

    def make_tile(block, q):
        scores = lax.dot_general(
            block, tgt_ref[...], (((1,), (1,)), ((), ())), preferred_element_type=F32
        )
        tile = jnp.exp2(scores * (LOG2_E / EPSILON)).astype(BF16)
        kernel[rows_of(q), :] = tile
        tile = tile.astype(F32)
        acc = lane_sums(lambda j: tile[:, j * 128:(j + 1) * 128])
        return lanes_to_row(acc)[0:1, :]

    def weigh_tile(q):
        acc = lane_sums(
            lambda j: kernel[rows_of(q), j * 128:(j + 1) * 128].astype(F32)
            * right[:, j * 128:(j + 1) * 128]
        )
        return lanes_to_row(acc)[0:1, :]

    def finish_left():
        @pl.loop(1, n_dev)
        def _(k):
            q = before(k)
            sum_copy(q, q).wait_recv()

        total = jnp.sum(inbox[...], axis=0)
        mass = src_mass_ref[:, pl.ds(pl.multiple_of(col * size, size), size)]
        left[:, rows_of(me)] = mass / total

        @pl.loop(1, n_dev)
        def _(k):
            left_copy(after(k), me).start()

        @pl.loop(1, n_dev)
        def _(k):
            q = before(k)
            left_copy(q, q).wait_recv()

        @pl.loop(1, n_dev)
        def _(k):
            q = after(k)
            sum_copy(q, me).wait_send()
            left_copy(q, me).wait_send()

    def right_scaling():
        weights = jnp.broadcast_to(left[...].astype(BF16), (8, left.shape[1]))
        cols = jnp.dot(weights, kernel[...], preferred_element_type=F32)
        mass = tgt_mass_ref[:, pl.ds(pl.multiple_of(row * own, own), own)]
        return mass / cols[0:1, :]

    inbox[me] = make_tile(src_ref[...], me)

    @pl.loop(1, n_dev)
    def _(k):
        q = before(k)
        gather_copy(q, q).wait_recv()
        part[:, rows_of(q)] = make_tile(src_all[rows_of(q), :], q)
        sum_copy(q, me).start()

    @pl.loop(1, n_dev)
    def _(k):
        gather_copy(after(k), me).wait_send()

    finish_left()

    @pl.loop(1, ITERS)
    def _(step):
        right[...] = right_scaling().astype(BF16).astype(F32)

        @pl.loop(1, n_dev)
        def _(k):
            q = before(k)
            part[:, rows_of(q)] = weigh_tile(q)
            sum_copy(q, me).start()

        inbox[me] = weigh_tile(me)
        finish_left()

    def out_block(r):
        return tgt_out.at[:, pl.ds(pl.multiple_of(r * own, own), own)]

    def out_copy(r, origin):
        return copy(out_block(origin), out_block(origin),
                    out_send.at[r], out_recv.at[origin], {"row": r, "col": col})

    tgt_out[:, pl.ds(pl.multiple_of(row * own, own), own)] = EPSILON * jnp.log(right_scaling())

    @pl.loop(1, n_row)
    def _(k):
        out_copy(lax.rem(row + k, n_row), row).start()

    span = n_col * size
    src_out[...] = EPSILON * jnp.log(left[:, pl.ds(pl.multiple_of(row * span, span), span)])

    @pl.loop(1, n_row)
    def _(k):
        r = lax.rem(row - k + n_row, n_row)
        out_copy(r, r).wait_recv()
        out_copy(lax.rem(row + k, n_row), row).wait_send()


def body(n_row, n_col, src_emb, tgt_emb, src_scale, tgt_scale, src_mass, tgt_mass):
    src_unit = unit_rows(src_emb, src_scale)
    tgt_unit = unit_rows(tgt_emb, tgt_scale)
    n_dev = n_row * n_col
    size, feat = src_emb.shape
    own = tgt_emb.shape[0]
    total = n_dev * size
    vmem = pl.BlockSpec(memory_space=pltpu.VMEM)
    dma = pltpu.SemaphoreType.DMA
    src_potential, tgt_potential = pl.pallas_call(
        functools.partial(sinkhorn, n_row, n_col),
        out_shape=(
            jax.ShapeDtypeStruct((1, n_col * size), F32),
            jax.ShapeDtypeStruct((1, n_row * own), F32),
        ),
        in_specs=[vmem] * 4,
        out_specs=(vmem, vmem),
        scratch_shapes=[
            pltpu.VMEM((total, feat), BF16),
            pltpu.VMEM((total, own), BF16),
            pltpu.VMEM((1, total), F32),
            pltpu.VMEM((n_dev, 1, size), F32),
            pltpu.VMEM((1, total), F32),
            pltpu.VMEM((1, own), F32),
            dma((n_dev,)), dma((n_dev,)), dma((n_dev,)), dma((n_dev,)),
            dma((n_dev,)), dma((n_dev,)), dma((n_row,)), dma((n_row,)),
        ],
        compiler_params=pltpu.CompilerParams(
            collective_id=0, has_side_effects=True, vmem_limit_bytes=56 * 2**20
        ),
        name="sinkhorn",
    )(src_unit, tgt_unit, src_mass[None, :], tgt_mass[None, :])
    return src_potential[0], tgt_potential[0]


def solution(mesh):
    in_specs = (
        P(("groups", "row", "col"), None),
        P(("groups", "col", "row"), None),
        P(("groups", "row", "col")),
        P(("groups", "col", "row")),
        P(("groups", "row")),
        P(("groups", "col")),
    )
    out_specs = (P(("groups", "row")), P(("groups", "col")))
    step = functools.partial(body, mesh.shape["row"], mesh.shape["col"])
    return jax.shard_map(step, mesh=mesh, in_specs=in_specs, out_specs=out_specs, check_vma=False)
```

time: 378 us -> 91.4 us (0.24)
  waiting for transfers between devices: 276 us -> 0 us
  Pallas kernels: 0 us -> 82.7 us
  matrix products: 66.8 us -> 0 us
  between operations: 13.8 us -> 0.69 us
  blocking collectives: 9.6 us -> 0 us
  other arithmetic: 10.7 us -> 4.98 us
    psum x3 -> x0, waiting for transfers between devices: 204 us -> none  [sum_cols(): return lax.psum(partial_cols, 'row')]
    pallas_call x0 -> x1, Pallas kernels: none -> 82.7 us  [body(): pl.pallas_call(functools.partial(sinkhorn, n_row, n_col), out_shape=(jax....]
    all_gather x1 -> x0, waiting for transfers between devices: 71.6 us -> none  [body(): lax.all_gather(tgt_unit, 'row', axis=0, tiled=True)]
    dot_general x7 -> x0, matrix products: 66.9 us -> none  [the longest x3 30.6 us: body(): jnp.dot(kernel, right_scaling.astype(jnp.bfloat16), preferred_element_typ...]
    psum x3 -> x0, blocking collectives: 7.6 us -> none  [sum_rows(): return lax.psum(partial_rows, 'col')]
  transfers between devices with their start and end apart: 4 -> 0, of which waited for: 4 -> 0; matrix products, arithmetic and copies ran while one was open for 1% -> 0% of each run, Pallas kernels for 0% -> 0%
where the time goes in v2:
time: 91.4 us; the launch traced here: 91.1 us
  Pallas kernels  82.7 us (90%)
  other arithmetic  4.98 us (5%)
  local copies, waits for them, and re-layouts  2.74 us (3%)
    pallas_call x1, Pallas kernels, body(): pl.pallas_call(functools.partial(sinkhorn, n_row, n_col), out_shape=(jax....  82.7 us
    unnamed x10, local copies, waits for them, and re-layouts  2.74 us
    reduce_sum x2, other arithmetic, unit_rows(): length = jnp.sqrt(jnp.sum(values * values, axis=1) + 1e-06)  2.43 us
    convert_element_type x2, other arithmetic, unit_rows(): return (values * (scale / length)[:, None]).astype(BF16)  1.86 us

profile of v2, /device:TPU:0, one launch (start us, length us, event | category | flops | bytes accessed | tf_op | source)
XLA Modules:
  0.0 91.1 jit_solution(1504917742103339908)
XLA Ops:
  0.6 0.0 copy-start
  0.6 1.0 %fusion.2 = f32[256]{0:T(256)S(1)} fusion(bf16[256,128]{1,0:T(8,128)(2,1)} %param.6), kind=kLoop, calls=%fused_computation.6 | loop fusion | flops 98048 | bytes 66560 | tf_op jit(solution)/shard_map/reduce_sum | solution.py:21
  1.7 0.7 rsqrt_multiply_fusion.1
  2.3 0.0 copy-start.2
  2.3 0.0 copy-start.1
  2.3 1.4 %fusion = f32[2048]{0:T(1024)S(1)} fusion(bf16[2048,128]{1,0:T(8,128)(2,1)} %param.7), kind=kLoop, calls=%fused_computation.2 | loop fusion | flops 784384 | bytes 532480 | tf_op jit(solution)/shard_map/reduce_sum | solution.py:21
  3.8 0.0 copy-done.2
  3.8 0.0 copy-done.1
  3.8 0.7 fusion.3.src_ref
  4.5 0.0 copy-done
  4.5 1.1 %fusion.1.tgt_ref = bf16[2048,128]{1,0:T(8,128)(2,1)} fusion(bf16[2048,128]{1,0:T(8,128)(2,1)S(1)} %copy-done, f32[2048]{0:T(1024)S(1)} %rsqrt_multiply_fusion), kind=kLoop, calls=%fused_computation.3 | loop fusion | flops 786432 | bytes 1056768 | tf_op jit(solution)/shard_map/convert_element_type | solution.py:22
  5.7 82.7 %sinkhorn.1 = (f32[1,512]{1,0:T(1,128)}, f32[1,16384]{1,0:T(1,128)}) custom-call(bf16[256,128]{1,0:T(8,128)(2,1)} %fusion.3.src_ref, bf16[2048,128]{1,0:T(8,128)(2,1)} %fusion.1.tgt_ref, f32[1,512]{1,0:T(1,128)} %bitcast.6, f32[1,16384]{1,0:T(1,128)} %bitcast.4), custom_call_target="tpu_custom_call" | custom-call | tf_op jit(solution)/shard_map/sinkhorn/pallas_call | solution.py:205
  88.4 0.0 copy-start.3
  88.4 0.7 copy-done.3
  89.1 0.6 copy.10
  89.6 1.5 %copy.11 = f32[16384]{0:T(1024)} copy(f32[16384]{0:T(1024)} %bitcast.5) | data formatting | bytes 131072
  (1 shorter events, 0.0 us)
Async XLA Ops:
  0.6 3.9 %copy-start = (bf16[2048,128]{1,0:T(8,128)(2,1)S(1)}, bf16[2048,128]{1,0:T(8,128)(2,1)}, u32[]{:S(2)}) copy-start(bf16[2048,128]{1,0:T(8,128)(2,1)} %param.7) | copy-start | bytes 1572868
  2.3 1.4 %copy-start.2 = (f32[2048]{0:T(1024)S(1)}, f32[2048]{0:T(1024)}, u32[]{:S(2)}) copy-start(f32[2048]{0:T(1024)} %param.9) | copy-start | bytes 24580
  2.3 1.5 %copy-start.1 = (bf16[256,128]{1,0:T(8,128)(2,1)S(1)}, bf16[256,128]{1,0:T(8,128)(2,1)}, u32[]{:S(2)}) copy-start(bf16[256,128]{1,0:T(8,128)(2,1)} %param.6) | copy-start | bytes 196612
  88.4 0.7 copy-start.3

commit v3 on v2

--- a/solution.py
+++ b/solution.py
@@ -14,12 +14,6 @@
 MESH = pl.DeviceIdType.MESH
 F32 = jnp.float32
 BF16 = jnp.bfloat16
-
-
-def unit_rows(emb, scale):
-    values = emb.astype(F32)
-    length = jnp.sqrt(jnp.sum(values * values, axis=1) + 1e-06)
-    return (values * (scale / length)[:, None]).astype(BF16)
 
 
 def lanes_to_row(acc):
@@ -34,13 +28,16 @@
 
 def sinkhorn(
     n_row, n_col,
-    src_ref, tgt_ref, src_mass_ref, tgt_mass_ref,
+    src_ref, tgt_ref, src_scale_ref, tgt_scale_ref, src_mass_ref, tgt_mass_ref,
     src_out, tgt_out,
-    src_all, kernel, part, inbox, left, right,
-    gather_send, gather_recv, sum_send, sum_recv, left_send, left_recv, out_send, out_recv,
+    src_all, tgt_all, kernel, part, inbox, left, right,
+    far_send, low_send, col_send, gather_recv, sum_send, sum_recv, left_send, left_recv, out_send, out_recv,
 ):
     n_dev = n_row * n_col
     row, col = lax.axis_index("row"), lax.axis_index("col")
+    n_low = 2 if n_row % 2 == 0 else 1
+    n_high = n_row // n_low
+    high, low = row // n_low, lax.rem(row, n_low)
     me = row * n_col + col
     size = src_ref.shape[0]
     own = tgt_ref.shape[0]
@@ -63,9 +60,9 @@
             device_id=device, device_id_type=MESH,
         )
 
-    def gather_copy(q, origin):
-        return copy(src_ref, src_all.at[rows_of(origin), :],
-                    gather_send.at[q], gather_recv.at[origin], peer(q))
+    def gather_copy(q, origin, send):
+        block = src_all.at[rows_of(origin), :]
+        return copy(block, block, send, gather_recv.at[origin], peer(q))
 
     def sum_copy(q, origin):
         return copy(part.at[:, rows_of(q)], inbox.at[origin],
@@ -75,18 +72,48 @@
         return copy(left.at[:, rows_of(origin)], left.at[:, rows_of(origin)],
                     left_send.at[q], left_recv.at[origin], peer(q))
 
+    def normalise(emb_ref, scale_ref, out_ref, start, count):
+        for j in range(count // 128):
+            values = emb_ref[j * 128:(j + 1) * 128, :].astype(F32)
+            squares = jnp.sum(values * values, axis=1, keepdims=True) + 1e-06
+            scale = jnp.broadcast_to(scale_ref[:, j * 128:(j + 1) * 128], (128, 128)).T
+            rows = pl.ds(pl.multiple_of(start + j * 128, 128), 128)
+            out_ref[rows, :] = (values * (scale / jnp.sqrt(squares))).astype(BF16)
+
     barrier = pltpu.get_barrier_semaphore()
 
     @pl.loop(1, n_dev)
     def _(k):
         pl.semaphore_signal(barrier, inc=1, device_id=peer(after(k)), device_id_type=MESH)
 
+    normalise(src_ref, src_scale_ref, src_all, me * size, size)
     pl.semaphore_wait(barrier, n_dev - 1)
 
-    @pl.loop(1, n_dev)
-    def _(k):
-        q = after(k)
-        gather_copy(q, me).start()
+    def at(high, low, column):
+        return (high * n_low + low) * n_col + column
+
+    def far_copy(k):
+        q = at(lax.rem(high + k, n_high), low, col)
+        return gather_copy(q, me, far_send.at[k])
+
+    def low_copy(k, origin):
+        q = at(high, lax.rem(low + k, n_low), col)
+        return gather_copy(q, origin, low_send.at[k, origin])
+
+    def col_copy(k, origin):
+        q = at(high, low, lax.rem(col + k, n_col))
+        return gather_copy(q, origin, col_send.at[k, origin])
+
+    @pl.loop(1, n_high)
+    def _(k):
+        far_copy(k).start()
+
+    for k in range(1, n_low):
+        low_copy(k, me).start()
+    for k in range(1, n_col):
+        col_copy(k, me).start()
+
+    normalise(tgt_ref, tgt_scale_ref, tgt_all, 0, own)
 
     def lane_sums(tile_of):
         acc = tile_of(0)
@@ -96,7 +123,7 @@
 
     def make_tile(block, q):
         scores = lax.dot_general(
-            block, tgt_ref[...], (((1,), (1,)), ((), ())), preferred_element_type=F32
+            block, tgt_all[...], (((1,), (1,)), ((), ())), preferred_element_type=F32
         )
         tile = jnp.exp2(scores * (LOG2_E / EPSILON)).astype(BF16)
         kernel[rows_of(q), :] = tile
@@ -142,18 +169,53 @@
         mass = tgt_mass_ref[:, pl.ds(pl.multiple_of(row * own, own), own)]
         return mass / cols[0:1, :]
 
-    inbox[me] = make_tile(src_ref[...], me)
-
-    @pl.loop(1, n_dev)
-    def _(k):
-        q = before(k)
-        gather_copy(q, q).wait_recv()
-        part[:, rows_of(q)] = make_tile(src_all[rows_of(q), :], q)
-        sum_copy(q, me).start()
-
-    @pl.loop(1, n_dev)
-    def _(k):
-        gather_copy(after(k), me).wait_send()
+    def use(origin):
+        part[:, rows_of(origin)] = make_tile(src_all[rows_of(origin), :], origin)
+        sum_copy(origin, me).start()
+
+    inbox[me] = make_tile(src_all[rows_of(me), :], me)
+
+    @pl.loop(1, n_high)
+    def _(k):
+        origin = at(lax.rem(high - k + n_high, n_high), low, col)
+        gather_copy(origin, origin, far_send.at[k]).wait_recv()
+        for j in range(1, n_low):
+            low_copy(j, origin).start()
+        for j in range(1, n_col):
+            col_copy(j, origin).start()
+        use(origin)
+
+    for i in range(1, n_low):
+        @pl.loop(0, n_high)
+        def _(k):
+            other = lax.rem(low - i + n_low, n_low)
+            origin = at(lax.rem(high - k + n_high, n_high), other, col)
+            gather_copy(origin, origin, far_send.at[0]).wait_recv()
+            for j in range(1, n_col):
+                col_copy(j, origin).start()
+            use(origin)
+
+    for i in range(1, n_col):
+        for l in range(n_low):
+            @pl.loop(0, n_high)
+            def _(k):
+                near = lax.rem(low - l + n_low, n_low)
+                column = lax.rem(col - i + n_col, n_col)
+                origin = at(lax.rem(high - k + n_high, n_high), near, column)
+                gather_copy(origin, origin, far_send.at[0]).wait_recv()
+                use(origin)
+
+    @pl.loop(1, n_high)
+    def _(k):
+        far_copy(k).wait_send()
+
+    @pl.loop(0, n_high)
+    def _(h):
+        for j in range(1, n_low):
+            low_copy(j, at(h, low, col)).wait_send()
+        for j in range(1, n_col):
+            for l in range(n_low):
+                col_copy(j, at(h, l, col)).wait_send()
 
     finish_left()
 
@@ -177,14 +239,14 @@
         return copy(out_block(origin), out_block(origin),
                     out_send.at[r], out_recv.at[origin], {"row": r, "col": col})
 
-    tgt_out[:, pl.ds(pl.multiple_of(row * own, own), own)] = EPSILON * jnp.log(right_scaling())
+    tgt_out[:, pl.ds(pl.multiple_of(row * own, own), own)] = right_scaling()
 
     @pl.loop(1, n_row)
     def _(k):
         out_copy(lax.rem(row + k, n_row), row).start()
 
     span = n_col * size
-    src_out[...] = EPSILON * jnp.log(left[:, pl.ds(pl.multiple_of(row * span, span), span)])
+    src_out[...] = left[:, pl.ds(pl.multiple_of(row * span, span), span)]
 
     @pl.loop(1, n_row)
     def _(k):
@@ -194,38 +256,41 @@
 
 
 def body(n_row, n_col, src_emb, tgt_emb, src_scale, tgt_scale, src_mass, tgt_mass):
-    src_unit = unit_rows(src_emb, src_scale)
-    tgt_unit = unit_rows(tgt_emb, tgt_scale)
     n_dev = n_row * n_col
     size, feat = src_emb.shape
     own = tgt_emb.shape[0]
     total = n_dev * size
     vmem = pl.BlockSpec(memory_space=pltpu.VMEM)
     dma = pltpu.SemaphoreType.DMA
-    src_potential, tgt_potential = pl.pallas_call(
+    left, right = pl.pallas_call(
         functools.partial(sinkhorn, n_row, n_col),
         out_shape=(
             jax.ShapeDtypeStruct((1, n_col * size), F32),
             jax.ShapeDtypeStruct((1, n_row * own), F32),
         ),
-        in_specs=[vmem] * 4,
+        in_specs=[vmem] * 6,
         out_specs=(vmem, vmem),
         scratch_shapes=[
             pltpu.VMEM((total, feat), BF16),
+            pltpu.VMEM((own, feat), BF16),
             pltpu.VMEM((total, own), BF16),
             pltpu.VMEM((1, total), F32),
             pltpu.VMEM((n_dev, 1, size), F32),
             pltpu.VMEM((1, total), F32),
             pltpu.VMEM((1, own), F32),
+            dma((n_row,)), dma((2, n_dev)), dma((n_col, n_dev)), dma((n_dev,)),
             dma((n_dev,)), dma((n_dev,)), dma((n_dev,)), dma((n_dev,)),
-            dma((n_dev,)), dma((n_dev,)), dma((n_row,)), dma((n_row,)),
+            dma((n_row,)), dma((n_row,)),
         ],
         compiler_params=pltpu.CompilerParams(
             collective_id=0, has_side_effects=True, vmem_limit_bytes=56 * 2**20
         ),
         name="sinkhorn",
-    )(src_unit, tgt_unit, src_mass[None, :], tgt_mass[None, :])
-    return src_potential[0], tgt_potential[0]
+    )(
+        src_emb, tgt_emb, src_scale[None, :], tgt_scale[None, :],
+        src_mass[None, :], tgt_mass[None, :],
+    )
+    return EPSILON * jnp.log(left[0]), EPSILON * jnp.log(right[0])
 
 
 def solution(mesh):

time: 91.4 us -> 75.3 us (0.82)
  Pallas kernels: 82.7 us -> 71.6 us
  other arithmetic: 4.98 us -> 2.15 us
  local copies, waits for them, and re-layouts: 2.74 us -> 0.68 us
    pallas_call x1, Pallas kernels: 82.7 us -> 71.6 us  [body(): pl.pallas_call(functools.partial(sinkhorn, n_row, n_col), out_shape=(jax....]
    reduce_sum x2 -> x0, other arithmetic: 2.43 us -> none  [unit_rows(): length = jnp.sqrt(jnp.sum(values * values, axis=1) + 1e-06)]
    mul x0 -> x2, other arithmetic: none -> 2.15 us  [body(): return (EPSILON * jnp.log(left[0]), EPSILON * jnp.log(right[0]))]
    unnamed x10 -> x2, local copies, waits for them, and re-layouts: 2.74 us -> 0.68 us
    convert_element_type x2 -> x0, other arithmetic: 1.86 us -> none  [unit_rows(): return (values * (scale / length)[:, None]).astype(BF16)]
where the time goes in v3:
time: 75.3 us; the launch traced here: 75.1 us
  Pallas kernels  71.6 us (95%)
  other arithmetic  2.15 us (3%)
    pallas_call x1, Pallas kernels, body(): pl.pallas_call(functools.partial(sinkhorn, n_row, n_col), out_shape=(jax....  71.6 us
    mul x2, other arithmetic, body(): return (EPSILON * jnp.log(left[0]), EPSILON * jnp.log(right[0]))  2.15 us

profile of v3, /device:TPU:0, one launch (start us, length us, event | category | flops | bytes accessed | tf_op | source)
XLA Modules:
  0.0 75.1 jit_solution(14666296353617066180)
XLA Ops:
  0.6 71.6 %sinkhorn.1 = (f32[1,512]{1,0:T(1,128)}, f32[1,16384]{1,0:T(1,128)}) custom-call(bf16[256,128]{1,0:T(8,128)(2,1)} %src_ref.1, bf16[2048,128]{1,0:T(8,128)(2,1)} %tgt_ref.1, f32[1,256]{1,0:T(1,128)} %bitcast.11, f32[1,2048]{1,0:T(1,128)} %bitcast.8, f32[1,512]{1,0:T(1,128)} %bitcast.9, f32[1,16384]{1,0:T(1,128)} %bitcast.7), custom_call_target="tpu_custom_call" | custom-call | tf_op jit(solution)/shard_map/sinkhorn/pallas_call | solution.py:265
  72.3 0.0 copy-start
  72.3 0.7 copy-done
  72.9 0.6 log_multiply_fusion.1
  73.5 1.6 %log_multiply_fusion = f32[1,16384]{1,0:T(1,128)} fusion(f32[1,16384]{1,0:T(1,128)} %get-tuple-element.5), kind=kLoop, calls=%fused_computation | loop fusion | flops 16384 | bytes 131072 | tf_op jit(solution)/shard_map/mul | solution.py:293
Async XLA Ops:
  72.3 0.7 copy-start

commit v4 on v3

--- a/solution.py
+++ b/solution.py
@@ -14,6 +14,10 @@
 MESH = pl.DeviceIdType.MESH
 F32 = jnp.float32
 BF16 = jnp.bfloat16
+
+
+def whole_sums_fit(n_dev, total):
+    return n_dev <= 16 and total % 4096 == 0
 
 
 def lanes_to_row(acc):
@@ -31,9 +35,15 @@
     src_ref, tgt_ref, src_scale_ref, tgt_scale_ref, src_mass_ref, tgt_mass_ref,
     src_out, tgt_out,
     src_all, tgt_all, kernel, part, inbox, left, right,
+    mass_all, part_rows, outbox, rows_inbox, mass_send, mass_recv, whole_send, whole_recv,
     far_send, low_send, col_send, gather_recv, sum_send, sum_recv, left_send, left_recv, out_send, out_recv,
 ):
     n_dev = n_row * n_col
+    unroll = n_dev - 1 if n_dev <= 16 else 1
+
+    def wrap(i, n):
+        return jnp.where(i >= n, i - n, i)
+
     row, col = lax.axis_index("row"), lax.axis_index("col")
     n_low = 2 if n_row % 2 == 0 else 1
     n_high = n_row // n_low
@@ -46,10 +56,10 @@
         return pl.ds(pl.multiple_of(q * size, size), size)
 
     def after(k):
-        return lax.rem(me + k, n_dev)
+        return wrap(me + k, n_dev)
 
     def before(k):
-        return lax.rem(me - k + n_dev, n_dev)
+        return wrap(me - k + n_dev, n_dev)
 
     def peer(q):
         return {"row": q // n_col, "col": lax.rem(q, n_col)}
@@ -65,12 +75,58 @@
         return copy(block, block, send, gather_recv.at[origin], peer(q))
 
     def sum_copy(q, origin):
-        return copy(part.at[:, rows_of(q)], inbox.at[origin],
-                    sum_send.at[q], sum_recv.at[origin], peer(q))
+        return copy(part.at[:, rows_of(q)], inbox.at[origin], sum_send, sum_recv, peer(q))
+
+    def all_sums():
+        others = inbox.at[pl.ds(0, n_dev - 1)]
+        return copy(others, others, sum_send, sum_recv, peer(after(1)))
+
+    whole_sums = whole_sums_fit(n_dev, n_dev * size)
+    lines = n_dev * size // 128
+    half = lines // 2
+
+    def whole_copy(q, origin, h, turn):
+        rows = pl.ds(h * half, half)
+        return copy(outbox.at[rows, :], rows_inbox.at[turn, origin, rows, :],
+                    whole_send.at[turn], whole_recv.at[turn], peer(q))
+
+    def all_wholes(turn):
+        others = rows_inbox.at[turn, pl.ds(0, n_dev - 1)]
+        return copy(others, others, whole_send.at[turn], whole_recv.at[turn], peer(after(1)))
+
+    def send_half(h, turn):
+        rows = slice(h * half, (h + 1) * half)
+        outbox[rows, :] = part_rows[rows, :].astype(BF16)
+
+        @pl.loop(1, n_dev, unroll=unroll)
+        def _(k):
+            whole_copy(after(k), me, h, turn).start()
+
+    def put_sums(q, sums):
+        if whole_sums:
+            for j in range(size // 128):
+                part_rows[pl.ds(q * (size // 128) + j, 1), :] = sums[:, j * 128:(j + 1) * 128]
+        else:
+            part[:, rows_of(q)] = sums
+            sum_copy(q, me).start()
+
+    def mass_copy(r, origin):
+        span = n_col * size
+        block = mass_all.at[:, pl.ds(pl.multiple_of(origin * span, span), span)]
+        return copy(src_mass_ref, block, mass_send, mass_recv, {"row": r, "col": col})
+
+    def all_masses():
+        others = mass_all.at[:, pl.ds(0, (n_row - 1) * n_col * size)]
+        return copy(others, others, mass_send, mass_recv,
+                    {"row": wrap(row + 1, n_row), "col": col})
+
+    def all_lefts():
+        others = left.at[:, pl.ds(0, (n_dev - 1) * size)]
+        return copy(others, others, left_send, left_recv, peer(after(1)))
 
     def left_copy(q, origin):
         return copy(left.at[:, rows_of(origin)], left.at[:, rows_of(origin)],
-                    left_send.at[q], left_recv.at[origin], peer(q))
+                    left_send, left_recv, peer(q))
 
     def normalise(emb_ref, scale_ref, out_ref, start, count):
         for j in range(count // 128):
@@ -82,7 +138,7 @@
 
     barrier = pltpu.get_barrier_semaphore()
 
-    @pl.loop(1, n_dev)
+    @pl.loop(1, n_dev, unroll=unroll)
     def _(k):
         pl.semaphore_signal(barrier, inc=1, device_id=peer(after(k)), device_id_type=MESH)
 
@@ -112,6 +168,14 @@
         low_copy(k, me).start()
     for k in range(1, n_col):
         col_copy(k, me).start()
+
+    if whole_sums:
+        span = n_col * size
+        mass_all[:, pl.ds(pl.multiple_of(row * span, span), span)] = src_mass_ref[...]
+
+        @pl.loop(1, n_row)
+        def _(k):
+            mass_copy(wrap(row + k, n_row), row).start()
 
     normalise(tgt_ref, tgt_scale_ref, tgt_all, 0, own)
 
@@ -138,30 +202,26 @@
         )
         return lanes_to_row(acc)[0:1, :]
 
-    def finish_left():
-        @pl.loop(1, n_dev)
-        def _(k):
-            q = before(k)
-            sum_copy(q, q).wait_recv()
-
+    def finish_left(turn):
+        if whole_sums:
+            rows_inbox[turn, me] = part_rows[...].astype(BF16)
+            all_wholes(turn).wait()
+            part_rows[...] = jnp.sum(rows_inbox[turn].astype(F32), axis=0)
+            for j in range(lines):
+                lanes = slice(j * 128, (j + 1) * 128)
+                left[:, lanes] = mass_all[:, lanes] / part_rows[j:j + 1, :]
+            return
+        all_sums().wait_recv()
         total = jnp.sum(inbox[...], axis=0)
         mass = src_mass_ref[:, pl.ds(pl.multiple_of(col * size, size), size)]
         left[:, rows_of(me)] = mass / total
 
-        @pl.loop(1, n_dev)
+        @pl.loop(1, n_dev, unroll=unroll)
         def _(k):
             left_copy(after(k), me).start()
 
-        @pl.loop(1, n_dev)
-        def _(k):
-            q = before(k)
-            left_copy(q, q).wait_recv()
-
-        @pl.loop(1, n_dev)
-        def _(k):
-            q = after(k)
-            sum_copy(q, me).wait_send()
-            left_copy(q, me).wait_send()
+        all_lefts().wait()
+        all_sums().wait_send()
 
     def right_scaling():
         weights = jnp.broadcast_to(left[...].astype(BF16), (8, left.shape[1]))
@@ -170,10 +230,12 @@
         return mass / cols[0:1, :]
 
     def use(origin):
-        part[:, rows_of(origin)] = make_tile(src_all[rows_of(origin), :], origin)
-        sum_copy(origin, me).start()
-
-    inbox[me] = make_tile(src_all[rows_of(me), :], me)
+        put_sums(origin, make_tile(src_all[rows_of(origin), :], origin))
+
+    if whole_sums:
+        put_sums(me, make_tile(src_all[rows_of(me), :], me))
+    else:
+        inbox[me] = make_tile(src_all[rows_of(me), :], me)
 
     @pl.loop(1, n_high)
     def _(k):
@@ -205,6 +267,11 @@
                 gather_copy(origin, origin, far_send.at[0]).wait_recv()
                 use(origin)
 
+    if whole_sums:
+        send_half(0, 0)
+        send_half(1, 0)
+        all_masses().wait()
+
     @pl.loop(1, n_high)
     def _(k):
         far_copy(k).wait_send()
@@ -217,42 +284,50 @@
             for l in range(n_low):
                 col_copy(j, at(h, l, col)).wait_send()
 
-    finish_left()
+    finish_left(0)
 
     @pl.loop(1, ITERS)
     def _(step):
+        turn = lax.rem(step, 2)
         right[...] = right_scaling().astype(BF16).astype(F32)
 
-        @pl.loop(1, n_dev)
-        def _(k):
-            q = before(k)
-            part[:, rows_of(q)] = weigh_tile(q)
-            sum_copy(q, me).start()
-
-        inbox[me] = weigh_tile(me)
-        finish_left()
+        if whole_sums:
+            for h in range(2):
+                @pl.loop(h * (n_dev // 2), (h + 1) * (n_dev // 2))
+                def _(q):
+                    put_sums(q, weigh_tile(q))
+
+                send_half(h, turn)
+        else:
+            @pl.loop(1, n_dev)
+            def _(k):
+                q = before(k)
+                put_sums(q, weigh_tile(q))
+
+            inbox[me] = weigh_tile(me)
+        finish_left(turn)
 
     def out_block(r):
         return tgt_out.at[:, pl.ds(pl.multiple_of(r * own, own), own)]
 
     def out_copy(r, origin):
         return copy(out_block(origin), out_block(origin),
-                    out_send.at[r], out_recv.at[origin], {"row": r, "col": col})
+                    out_send, out_recv, {"row": r, "col": col})
+
+    def all_outs():
+        others = tgt_out.at[:, pl.ds(0, (n_row - 1) * own)]
+        return copy(others, others, out_send, out_recv, {"row": wrap(row + 1, n_row), "col": col})
 
     tgt_out[:, pl.ds(pl.multiple_of(row * own, own), own)] = right_scaling()
 
-    @pl.loop(1, n_row)
-    def _(k):
-        out_copy(lax.rem(row + k, n_row), row).start()
+    @pl.loop(1, n_row, unroll=min(unroll, n_row - 1))
+    def _(k):
+        out_copy(wrap(row + k, n_row), row).start()
 
     span = n_col * size
     src_out[...] = left[:, pl.ds(pl.multiple_of(row * span, span), span)]
 
-    @pl.loop(1, n_row)
-    def _(k):
-        r = lax.rem(row - k + n_row, n_row)
-        out_copy(r, r).wait_recv()
-        out_copy(lax.rem(row + k, n_row), row).wait_send()
+    all_outs().wait()
 
 
 def body(n_row, n_col, src_emb, tgt_emb, src_scale, tgt_scale, src_mass, tgt_mass):
@@ -260,6 +335,8 @@
     size, feat = src_emb.shape
     own = tgt_emb.shape[0]
     total = n_dev * size
+    whole_sums = whole_sums_fit(n_dev, total)
+    lines = total // 128 if whole_sums else 16
     vmem = pl.BlockSpec(memory_space=pltpu.VMEM)
     dma = pltpu.SemaphoreType.DMA
     left, right = pl.pallas_call(
@@ -278,9 +355,13 @@
             pltpu.VMEM((n_dev, 1, size), F32),
             pltpu.VMEM((1, total), F32),
             pltpu.VMEM((1, own), F32),
+            pltpu.VMEM((1, total if whole_sums else 128), F32),
+            pltpu.VMEM((lines, 128), F32),
+            pltpu.VMEM((lines, 128), BF16),
+            pltpu.VMEM((2, n_dev if whole_sums else 1, lines, 128), BF16),
+            dma, dma, dma((2,)), dma((2,)),
             dma((n_row,)), dma((2, n_dev)), dma((n_col, n_dev)), dma((n_dev,)),
-            dma((n_dev,)), dma((n_dev,)), dma((n_dev,)), dma((n_dev,)),
-            dma((n_row,)), dma((n_row,)),
+            dma, dma, dma, dma, dma, dma,
         ],
         compiler_params=pltpu.CompilerParams(
             collective_id=0, has_side_effects=True, vmem_limit_bytes=56 * 2**20

time: 75.3 us -> 64.1 us (0.85)
  Pallas kernels: 71.6 us -> 60.4 us
    pallas_call x1, Pallas kernels: 71.6 us -> 60.4 us  [body(): pl.pallas_call(functools.partial(sinkhorn, n_row, n_col), out_shape=(jax....]
where the time goes in v4:
time: 64.1 us; the launch traced here: 63.8 us
  Pallas kernels  60.4 us (94%)
  other arithmetic  2.15 us (3%)
  local copies, waits for them, and re-layouts  0.68 us (1%)
  between operations  0.65 us (1%)
    pallas_call x1, Pallas kernels, body(): pl.pallas_call(functools.partial(sinkhorn, n_row, n_col), out_shape=(jax....  60.4 us
    mul x2, other arithmetic, body(): return (EPSILON * jnp.log(left[0]), EPSILON * jnp.log(right[0]))  2.15 us

profile of v4, /device:TPU:0, one launch (start us, length us, event | category | flops | bytes accessed | tf_op | source)
XLA Modules:
  0.0 63.8 jit_solution(17016527766263640354)
XLA Ops:
  0.6 60.4 %sinkhorn.1 = (f32[1,512]{1,0:T(1,128)}, f32[1,16384]{1,0:T(1,128)}) custom-call(bf16[256,128]{1,0:T(8,128)(2,1)} %src_ref.1, bf16[2048,128]{1,0:T(8,128)(2,1)} %tgt_ref.1, f32[1,256]{1,0:T(1,128)} %bitcast.11, f32[1,2048]{1,0:T(1,128)} %bitcast.8, f32[1,512]{1,0:T(1,128)} %bitcast.9, f32[1,16384]{1,0:T(1,128)} %bitcast.7), custom_call_target="tpu_custom_call" | custom-call | tf_op jit(solution)/shard_map/sinkhorn/pallas_call | solution.py:342
  61.0 0.0 copy-start
  61.0 0.7 %copy-done = f32[1,512]{1,0:T(1,128)S(1)} copy-done((f32[1,512]{1,0:T(1,128)S(1)}, f32[1,512]{1,0:T(1,128)}, u32[]{:S(2)}) %copy-start) | copy-done | bytes 2072
  61.7 0.6 log_multiply_fusion.1
  62.3 1.6 %log_multiply_fusion = f32[1,16384]{1,0:T(1,128)} fusion(f32[1,16384]{1,0:T(1,128)} %get-tuple-element.5), kind=kLoop, calls=%fused_computation | loop fusion | flops 16384 | bytes 131072 | tf_op jit(solution)/shard_map/mul | solution.py:374
Async XLA Ops:
  61.0 0.7 %copy-start = (f32[1,512]{1,0:T(1,128)S(1)}, f32[1,512]{1,0:T(1,128)}, u32[]{:S(2)}) copy-start(f32[1,512]{1,0:T(1,128)} %get-tuple-element.4) | copy-start | bytes 6148

commit v5 on v4

--- a/solution.py
+++ b/solution.py
@@ -293,7 +293,7 @@
 
         if whole_sums:
             for h in range(2):
-                @pl.loop(h * (n_dev // 2), (h + 1) * (n_dev // 2))
+                @pl.loop(h * (n_dev // 2), (h + 1) * (n_dev // 2), unroll=8)
                 def _(q):
                     put_sums(q, weigh_tile(q))
 

time: 64.1 us -> 59.1 us (0.922)
  Pallas kernels: 60.4 us -> 55.4 us
    pallas_call x1, Pallas kernels: 60.4 us -> 55.4 us  [body(): pl.pallas_call(functools.partial(sinkhorn, n_row, n_col), out_shape=(jax....]
where the time goes in v5:
time: 59.1 us; the launch traced here: 58.9 us
  Pallas kernels  55.4 us (94%)
  other arithmetic  2.15 us (4%)
  local copies, waits for them, and re-layouts  0.68 us (1%)
  between operations  0.65 us (1%)
    pallas_call x1, Pallas kernels, body(): pl.pallas_call(functools.partial(sinkhorn, n_row, n_col), out_shape=(jax....  55.4 us
    mul x2, other arithmetic, body(): return (EPSILON * jnp.log(left[0]), EPSILON * jnp.log(right[0]))  2.15 us

profile of v5, /device:TPU:0, one launch (start us, length us, event | category | flops | bytes accessed | tf_op | source)
XLA Modules:
  0.0 58.9 jit_solution(14240180951872319786)
XLA Ops:
  0.6 55.4 %sinkhorn.1 = (f32[1,512]{1,0:T(1,128)}, f32[1,16384]{1,0:T(1,128)}) custom-call(bf16[256,128]{1,0:T(8,128)(2,1)} %src_ref.1, bf16[2048,128]{1,0:T(8,128)(2,1)} %tgt_ref.1, f32[1,256]{1,0:T(1,128)} %bitcast.11, f32[1,2048]{1,0:T(1,128)} %bitcast.8, f32[1,512]{1,0:T(1,128)} %bitcast.9, f32[1,16384]{1,0:T(1,128)} %bitcast.7), custom_call_target="tpu_custom_call" | custom-call | tf_op jit(solution)/shard_map/sinkhorn/pallas_call | solution.py:342
  56.1 0.0 copy-start
  56.1 0.7 %copy-done = f32[1,512]{1,0:T(1,128)S(1)} copy-done((f32[1,512]{1,0:T(1,128)S(1)}, f32[1,512]{1,0:T(1,128)}, u32[]{:S(2)}) %copy-start) | copy-done | bytes 2072
  56.8 0.6 log_multiply_fusion.1
  57.3 1.6 %log_multiply_fusion = f32[1,16384]{1,0:T(1,128)} fusion(f32[1,16384]{1,0:T(1,128)} %get-tuple-element.5), kind=kLoop, calls=%fused_computation | loop fusion | flops 16384 | bytes 131072 | tf_op jit(solution)/shard_map/mul | solution.py:374
Async XLA Ops:
  56.1 0.7 %copy-start = (f32[1,512]{1,0:T(1,128)S(1)}, f32[1,512]{1,0:T(1,128)}, u32[]{:S(2)}) copy-start(f32[1,512]{1,0:T(1,128)} %get-tuple-element.4) | copy-start | bytes 6148
